TPU v7x, 32 devices: a whole 2x2x4 slice. The times are simulated.
32 devices in a mesh: gx: 4 (over y, core), gy: 4 (over z), gz: 2 (over x).
Axes of the slice: x: 2, y: 2, z: 4, core: 2. Of those that a mesh axis runs over, the one named last changes fastest.
Arguments:
- positions: float32 [4, 4, 2, 3, 256], P('gx', 'gy', 'gz'), may hold values from 0.3 to 7.7, as said below
- velocities: float32 [4, 4, 2, 3, 256], P('gx', 'gy', 'gz'), may hold values from -6 to 6
- species: int32 [4, 4, 2, 256], P('gx', 'gy', 'gz'), may hold values from 0 to 3
- pair_table: int32 [4, 4, 2, 3, 1536], P('gx', 'gy', 'gz'), may hold values from 0 to 6911, as said below
- live_blocks: int32 [4, 4, 2], P('gx', 'gy', 'gz'), may hold values from 6 to 12, as said below
- owners: int32 [4, 4, 2, 2], P('gx', 'gy', 'gz'), may hold values from 0 to 1, as said below
- radial_weight: float32 [256, 8], replicated, may hold values from -2 to 2
- center_embed: float32 [256, 4], replicated, may hold values from -3 to 3
- neighbour_embed: float32 [256, 4], replicated, may hold values from -3 to 3
- vector_weight: float32 [32, 8], replicated, may hold values from -2 to 2
- env_weight: float32 [2, 32, 256], replicated, may hold values from -0.375 to 0.375
- vector_gate: float32 [32, 256], replicated, may hold values from -0.375 to 0.375
- latent_weight: float32 [2, 256, 288], replicated, may hold values from -0.375 to 0.375
- energy_weight: float32 [256], replicated, may hold values from -0.375 to 0.375
Outputs:
- migrated: float32 [4, 4, 2, 2, 9, 128], P('gx', 'gy', 'gz')
Inputs may be any that keep to these rules, and one draw needn't show every extreme that they name: `positions`: atom k of a domain lies within 0.2 in each coordinate of the point (ix + 0.5, iy + 0.5, iz + 0.5) with k = (8 ix + iy) (4) + iz. `pair_table`: row 0 is a centre atom index below 256; row 1 a neighbour index as in the statement, never the centre itself; row 2 equals the species of that neighbour atom in its own domain. `live_blocks`: some device uses all 12 blocks. The owners of one device's blocks are distinct; in every gz group some device is the owner of one block of every device of the group.
All inputs are finite; a program needn't handle non-finite values.
Results may differ from a plain program's by a relative error of at most 0.0003.
Values sent between devices are 32-bit elements; how exact they have to be, the bound alone decides.
A program may use at most 64 MiB of HBM per device.

v0:
```python
import functools

import jax
import jax.numpy as jnp
from jax import lax
from jax.experimental import pallas as pl
from jax.experimental.pallas import tpu as pltpu
from jax.sharding import PartitionSpec as P

CUTOFF = 5.0
ENV_SCALE = 0.4
TIME_STEP = 0.2
CHUNK = 256
SLOTS = 27
F32 = jnp.float32
BF16 = jnp.bfloat16
MESH = pl.DeviceIdType.MESH


def split(x):
    high = x.astype(BF16)
    return high, (x - high.astype(F32)).astype(BF16)


def split3(x):
    high = x.astype(BF16)
    rest = x - high.astype(F32)
    mid = rest.astype(BF16)
    return high, mid, (rest - mid.astype(F32)).astype(BF16)


def dot(a, b):
    return jnp.dot(a, b, preferred_element_type=F32)


def dot_t(a, b):
    return lax.dot_general(a, b, (((1,), (1,)), ((), ())), preferred_element_type=F32)


def mul3(w_high, w_low, x):
    high, low = split(x)
    return dot(w_high, high) + dot(w_high, low) + dot(w_low, high)


def wide(x, lanes):
    if x.shape[1] == lanes:
        return x
    return jnp.concatenate([x, jnp.zeros((x.shape[0], lanes - x.shape[1]), x.dtype)], axis=1)


def tall(x, rows):
    if x.shape[0] == rows:
        return x
    return jnp.concatenate([x, jnp.zeros((rows - x.shape[0], x.shape[1]), x.dtype)], axis=0)


def stack3(x):
    high, low = split(x)
    rows = 3 * x.shape[0]
    pad = -rows % 128
    parts = [high.astype(F32), low.astype(F32), high.astype(F32)]
    if pad:
        parts.append(jnp.zeros((pad, x.shape[1]), F32))
    return jnp.concatenate(parts, axis=0).astype(BF16)


def pack3(transposed):
    high, low = split(transposed)
    high, low = high.astype(F32), low.astype(F32)
    rows = 3 * transposed.shape[0]
    stacked = tall(jnp.concatenate([high, high, low], axis=0), rows + (-rows % 128))
    return stacked.T.astype(BF16)


def silu_pair(x):
    gate = 0.5 + 0.5 * jnp.tanh(0.5 * x)
    value = x * gate
    return value, gate + value * (1.0 - gate)


def rows3(x):
    n = x.shape[0] // 3
    return x[:n], x[n : 2 * n], x[2 * n :]


def prepare(weights, scratch):
    radial, centre_e, neigh_e, vector, env_w, gate_w, latent_w, energy = weights
    (w_first, wa_h, wa_l, wb_h, wb_l, s0, s1, t0_h, t0_l, t1_h, t1_l, gate_t, e0_t, e1_t, back_h, back_l, ew) = scratch
    width = radial.shape[0]
    channels = vector.shape[0]
    radial_t = wide(radial[...], 128).T[:8]
    centre_t = wide(centre_e[...], 128).T[:8]
    neigh_t = wide(neigh_e[...], 128).T[:8]
    vector_t = wide(tall(vector[...], 128), 128).T[:8, :channels]
    zeros = jnp.zeros((8, 128), F32)
    vector_tp = wide(vector_t, 128)
    first_t = jnp.concatenate(
        [
            jnp.concatenate([radial_t, vector_tp], axis=1),
            jnp.concatenate([centre_t, zeros], axis=1),
            jnp.concatenate([neigh_t, zeros], axis=1),
        ],
        axis=0,
    )
    w_first[...] = pack3(first_t)
    layer0 = wide(latent_w[0], 384).T
    layer1 = wide(latent_w[1], 384).T
    high, low = split(jnp.concatenate([latent_w[0][:, :width], gate_w[...], env_w[0]], axis=0))
    wa_h[...], wa_l[...] = high, low
    high, low = split(jnp.concatenate([latent_w[1][:, :width], env_w[1]], axis=0))
    wb_h[...], wb_l[...] = high, low
    s0[...] = pack3(layer0[width : width + channels])
    s1[...] = pack3(layer1[width : width + channels])
    t0_h[...], t0_l[...] = split(layer0[: width + channels])
    t1_h[...], t1_l[...] = split(layer1[: width + channels])
    gate_t[...] = pack3(gate_w[...])
    e0_t[...] = pack3(env_w[0])
    e1_t[...] = pack3(env_w[1])
    back = tall(jnp.concatenate([radial_t, vector_tp], axis=1), 16)
    back_h[...], back_l[...] = split(back)
    ew[...] = jnp.broadcast_to(tall(energy[...], 8).T[:, :1], (width, 128))


def hot_matrices(pair, mem_t, nbr_t, atoms):
    count = pair.shape[1]
    labels = lax.broadcasted_iota(jnp.int32, (atoms, CHUNK), 0)

    def chunk(i, carry):
        here = pl.ds(pl.multiple_of(i * CHUNK, CHUNK), CHUNK)
        centre = pair[0:1, here]
        atom = pair[1:2, here] & (atoms - 1)
        mem_t[:, here] = (labels == centre).astype(F32).astype(BF16)
        nbr_t[:, here] = (labels == atom).astype(F32).astype(BF16)
        return carry

    lax.fori_loop(0, count // CHUNK, chunk, 0)


def sum3(values, by):
    a, b, c = rows3(values)
    return a * by[0:1] + b * by[1:2] + c * by[2:3]


def times3(by, value):
    return jnp.concatenate([value * by[0:1], value * by[1:2], value * by[2:3]], axis=0)


def tile3(value):
    return jnp.concatenate([value, value, value], axis=0)


def fold3(values):
    a, b, c = rows3(values)
    return a + b + c


def sums3(values):
    a, b, c = rows3(values)
    return jnp.concatenate(
        [jnp.sum(a, axis=0, keepdims=True), jnp.sum(b, axis=0, keepdims=True), jnp.sum(c, axis=0, keepdims=True)],
        axis=0,
    )


def gradient(table, near_table, pair, live, weights, hots, store):
    (w_first, wa_h, wa_l, wb_h, wb_l, s0, s1, t0_h, t0_l, t1_h, t1_l, gate_t, e0_t, e1_t, back_h, back_l, ew) = weights
    mem_t, nbr_t = hots
    (geo, trig, silu0, dsilu0, upper, lower, silu1, dsilu1, small, at0s, v1s, dv1s, dlat, acc, spread_acc) = store
    atoms, count = mem_t.shape
    depth = float(atoms // 64)
    width = silu0.shape[0]
    ch = v1s.shape[0] // 3
    steps = count // CHUNK
    slot_rows = lax.broadcasted_iota(jnp.int32, (32, CHUNK), 0)
    lanes = lax.broadcasted_iota(jnp.int32, (1, CHUNK), 1)
    orders = (lax.broadcasted_iota(jnp.int32, (8, CHUNK), 0) + 1).astype(F32)
    kinds = lax.broadcasted_iota(jnp.int32, (8, CHUNK), 0)
    vw, vb, g0, ep0, ep1, dvw = (slice(k * ch, (k + 1) * ch) for k in range(6))

    def at(i):
        return pl.ds(pl.multiple_of(i * CHUNK, CHUNK), CHUNK)

    def loop(body):
        acc[...] = jnp.zeros_like(acc)
        lax.fori_loop(0, steps, lambda i, c: (body(at(i), i), c)[1], 0)
        total = acc[...]
        n = total.shape[0] // 2
        high, low = split(ENV_SCALE * (total[:n] + total[n:]))
        return jnp.concatenate([high, low], axis=0)

    def gather(two, here):
        both = dot(two, mem_t[:, here])
        n = both.shape[0] // 2
        return both[:n] + both[n:]

    def scatter(values, here):
        high, low = split(values)
        acc[...] += dot_t(jnp.concatenate([high, low], axis=0), mem_t[:, here])

    def energy_rows():
        value = ew[...]
        return jnp.concatenate([value] * (CHUNK // 128), axis=1)

    def phase_a(here, i):
        slot = pair[1:2, here] // atoms
        far = dot(table, nbr_t[:, here])
        far = far[:96] + far[96:192] + far[192:]
        hot = slot_rows == slot
        picks = [
            jnp.sum(jnp.where(hot, far[32 * m : 32 * m + 32], 0.0), axis=0, keepdims=True) for m in range(3)
        ]
        near = dot(near_table, mem_t[:, here])
        centre_hot = near[24:32]
        near = near[0:8] + near[8:16] + near[16:24]
        shift_x = (slot // 9 - 1).astype(F32) * 8.0
        shift_y = (slot // 3 % 3 - 1).astype(F32) * 8.0
        shift_z = (slot % 3 - 1).astype(F32) * depth
        dx = picks[0] + shift_x - near[0:1]
        dy = picks[1] + shift_y - near[1:2]
        dz = picks[2] + shift_z - near[2:3]
        distance = jnp.sqrt(dx * dx + dy * dy + dz * dz)
        inverse = 1.0 / distance
        unit = jnp.concatenate([dx, dy, dz], axis=0) * inverse
        ratio = distance / CUTOFF
        use = (i * CHUNK + lanes < live * 128).astype(F32)
        bump = 1.0 - ratio * ratio
        envelope = bump * bump * use
        slope = bump * use * (-4.0 / CUTOFF) * ratio
        angle = orders * jnp.pi * distance / CUTOFF
        norm = (2.0 / CUTOFF) ** 0.5 * inverse
        basis = norm * jnp.sin(angle)
        trig[:, here] = norm * (orders * (jnp.pi / CUTOFF)) * jnp.cos(angle) - basis * inverse
        geo[0:3, here] = unit
        geo[3:4, here] = envelope
        geo[4:5, here] = inverse
        geo[5:6, here] = slope
        other_hot = (kinds == pair[2:3, here]).astype(F32)
        first = dot(w_first[...], stack3(jnp.concatenate([basis, centre_hot, other_hot], axis=0)))
        value, deriv = silu_pair(first[:width])
        silu0[:, here] = value
        dsilu0[:, here] = deriv
        plain = first[width : width + ch]
        small[vb, here] = plain
        small[vw, here] = envelope * plain
        after = mul3(wa_h[...], wa_l[...], envelope * value)
        upper[:, here] = after[:width]
        small[g0, here] = after[width : width + ch]
        small[ep0, here] = after[width + ch :]
        scatter(times3(unit, after[width + ch :]), here)

    env0 = loop(phase_a)

    def phase_b(here, i):
        unit, envelope = geo[0:3, here], geo[3:4, here]
        at_pairs = gather(env0, here)
        at0s[:, here] = at_pairs
        vw_here = small[vw, here]
        scalars = vw_here * sum3(at_pairs, unit)
        update = upper[:, here] + dot(s0[...], stack3(scalars))
        value, deriv = silu_pair(update)
        silu1[:, here] = value
        dsilu1[:, here] = deriv
        v1s[:, here] = times3(unit, vw_here) + at_pairs * tile3(small[g0, here])
        after = mul3(wb_h[...], wb_l[...], envelope * (silu0[:, here] + value))
        lower[:, here] = after[:width]
        small[ep1, here] = after[width:]
        scatter(times3(unit, after[width:]), here)

    env1 = loop(phase_b)

    def phase_c(here, i):
        envelope = geo[3:4, here]
        at_pairs = gather(env1, here)
        vectors = v1s[:, here]
        update = lower[:, here] + dot(s1[...], stack3(fold3(vectors * at_pairs)))
        value, deriv = silu_pair(update)
        weight = energy_rows()
        geo[6:7, here] = jnp.sum(weight * value, axis=0, keepdims=True)
        back = mul3(t1_h[...], t1_l[...], weight * deriv * envelope)
        dlat[:, here] = weight + back[:width]
        d_scalar = tile3(back[width:])
        dv1s[:, here] = d_scalar * at_pairs
        scatter(d_scalar * vectors, here)

    denv1 = loop(phase_c)

    def phase_d(here, i):
        unit, envelope = geo[0:3, here], geo[3:4, here]
        d_spread = gather(denv1, here)
        d_unit = sums3(d_spread * tile3(small[ep1, here]))
        at_pairs = at0s[:, here]
        dv1 = dv1s[:, here]
        d_latent = dlat[:, here] + dot(e1_t[...], stack3(sum3(d_spread, unit)))
        d_gate = fold3(dv1 * at_pairs)
        back = mul3(t0_h[...], t0_l[...], d_latent * envelope * dsilu1[:, here])
        geo[6:7, here] = geo[6:7, here] + jnp.sum(d_latent * silu1[:, here], axis=0, keepdims=True)
        dlat[:, here] = d_latent + back[:width] + dot(gate_t[...], stack3(d_gate))
        d_scalar = back[width:]
        vw_here = small[vw, here]
        d_vectors = dv1 + tile3(d_scalar) * at_pairs
        small[dvw, here] = sum3(d_vectors, unit)
        geo[8:11, here] = d_unit + sums3(d_vectors * tile3(vw_here))
        scatter(dv1 * tile3(small[g0, here]) + times3(unit, d_scalar * vw_here), here)

    denv0 = loop(phase_d)
    spread_acc[...] = jnp.zeros_like(spread_acc)

    def phase_e(here, i):
        unit, envelope = geo[0:3, here], geo[3:4, here]
        d_spread = gather(denv0, here)
        d_unit = geo[8:11, here] + sums3(d_spread * tile3(small[ep0, here]))
        d_latent = dlat[:, here] + dot(e0_t[...], stack3(sum3(d_spread, unit)))
        d_vw = small[dvw, here]
        d_envelope = (
            geo[6:7, here]
            + jnp.sum(d_latent * silu0[:, here], axis=0, keepdims=True)
            + jnp.sum(d_vw * small[vb, here], axis=0, keepdims=True)
        )
        d_first = jnp.concatenate(
            [d_latent * envelope * dsilu0[:, here], tall(envelope * d_vw, 128)], axis=0
        )
        d_basis = mul3(back_h[...], back_l[...], d_first)[:8]
        d_distance = jnp.sum(d_basis * trig[:, here], axis=0, keepdims=True) + d_envelope * geo[5:6, here]
        along = jnp.sum(unit * d_unit, axis=0, keepdims=True)
        d_move = unit * d_distance + (d_unit - unit * along) * geo[4:5, here]
        hot = slot_rows == pair[1:2, here] // atoms
        high, low = split(
            jnp.concatenate([jnp.where(hot, d_move[m : m + 1], 0.0) for m in range(3)], axis=0)
        )
        spread_acc[0:192] += dot_t(jnp.concatenate([high, low], axis=0), nbr_t[:, here])
        high, low = split(tall(d_move, 16))
        spread_acc[192:224] += dot_t(jnp.concatenate([high, low], axis=0), mem_t[:, here])

    lax.fori_loop(0, steps, lambda i, c: (phase_e(at(i), i), c)[1], 0)
    by_slot = spread_acc[0:96] + spread_acc[96:192]
    by_centre = spread_acc[192:208] + spread_acc[208:224]
    return by_slot, by_centre


def weight_scratch(width, ch):
    def b(*shape):
        return pltpu.VMEM(shape, BF16)

    return [
        b(width + 128, 128),
        b(width + 2 * ch, width),
        b(width + 2 * ch, width),
        b(width + ch, width),
        b(width + ch, width),
        b(width, 128),
        b(width, 128),
        b(width + ch, width),
        b(width + ch, width),
        b(width + ch, width),
        b(width + ch, width),
        b(width, 128),
        b(width, 128),
        b(width, 128),
        b(16, width + 128),
        b(16, width + 128),
        pltpu.VMEM((width, 128), F32),
    ]


def store_scratch(width, ch, count, atoms):
    def f(*shape):
        return pltpu.VMEM(shape, F32)

    return [
        f(16, count),
        f(8, count),
        f(width, count),
        f(width, count),
        f(width, count),
        f(width, count),
        f(width, count),
        f(width, count),
        f(6 * ch, count),
        f(3 * ch, count),
        f(3 * ch, count),
        f(3 * ch, count),
        f(width, count),
        f(6 * ch, atoms),
        f(224, atoms),
    ]


def wrapped(step, size):
    return step % size


def kernel(
    sizes,
    live_ref,
    owner_ref,
    pos,
    vel,
    kind,
    pair,
    radial,
    centre_e,
    neigh_e,
    vector,
    env_w,
    gate_w,
    latent_w,
    energy,
    out,
    *scratch,
):
    xs, ys, zs = sizes
    weights = (radial, centre_e, neigh_e, vector, env_w, gate_w, latent_w, energy)
    w_scratch, store = scratch[:17], scratch[17:32]
    (mem_t, nbr_t, own, halo, force_out, force_in, move_out, move_in,
     pos_send, pos_recv, force_send, force_recv, move_send, move_recv) = scratch[32:]
    atoms = pos.shape[1]
    me = (lax.axis_index("gx"), lax.axis_index("gy"), lax.axis_index("gz"))

    def device(step):
        return tuple(lax.rem(m + s % n, n) for m, s, n in zip(me, step, sizes))

    slots = [(x, y, z) for x in (-1, 0, 1) for y in (-1, 0, 1) for z in (-1, 0, 1)]
    first = {}
    for k, s in enumerate(slots):
        first.setdefault((s[0] % xs, s[1] % ys, s[2] % zs), k)
    leader = [first[(s[0] % xs, s[1] % ys, s[2] % zs)] for s in slots]
    home = first[(0, 0, 0)]
    leaders = [k for k in first.values() if k != home]
    partners = {(s[0] % xs, s[1] % ys, s[2] % zs) for s in (slots[k] for k in leaders)}
    partners |= {((-x) % xs, (-y) % ys, (-z) % zs) for x, y, z in partners}
    partners |= {(0, 0, z) for z in range(1, zs)}
    partners = sorted(partners)

    barrier = pltpu.get_barrier_semaphore()
    for step in partners:
        pl.semaphore_signal(barrier, inc=1, device_id=device(step), device_id_type=MESH)
    here = pos[...]
    for m in range(3):
        own[0, :, m * atoms : (m + 1) * atoms] = here[m : m + 1]
    pl.semaphore_wait(barrier, len(partners))

    def push(k, source, target, send, recv, step):
        return pltpu.make_async_remote_copy(
            src_ref=source, dst_ref=target, send_sem=send.at[k], recv_sem=recv.at[k],
            device_id=device(step), device_id_type=MESH,
        )

    pos_copies = [
        push(k, own.at[0], halo.at[k], pos_send, pos_recv, tuple(-v for v in slots[k])) for k in leaders
    ]
    for copy in pos_copies:
        copy.start()

    prepare(weights, w_scratch)
    hot_matrices(pair, mem_t, nbr_t, atoms)
    species_hot = (
        lax.broadcasted_iota(jnp.int32, (8, atoms), 0) == kind[...]
    ).astype(F32)
    high, mid, low = (v.astype(F32) for v in split3(tall(here, 8)))
    near_table = jnp.concatenate([high, mid, low, species_hot], axis=0).astype(BF16)

    for copy in pos_copies:
        copy.wait()
    rows = []
    for m in range(3):
        cut = slice(m * atoms, (m + 1) * atoms)
        for k in range(SLOTS):
            rows.append(own[0, :, cut] if leader[k] == home else halo[leader[k], :, cut])
        rows.append(jnp.zeros((32 - SLOTS, atoms), F32))
    table = jnp.concatenate(split3(jnp.concatenate(rows, axis=0)), axis=0)

    by_slot, by_centre = gradient(
        table, near_table, pair, live_ref[0], w_scratch, (mem_t, nbr_t), store
    )

    members = {k: [j for j in range(SLOTS) if leader[j] == k] for k in leaders + [home]}

    def piece(k):
        parts = []
        for m in range(3):
            row = by_slot[32 * m + k : 32 * m + k + 1]
            for j in members[k][1:]:
                row = row + by_slot[32 * m + j : 32 * m + j + 1]
            parts.append(row)
        return parts

    force_copies = []
    for k in leaders:
        for m, row in enumerate(piece(k)):
            force_out[k, :, m * atoms : (m + 1) * atoms] = row
        copy = push(k, force_out.at[k], force_in.at[k], force_send, force_recv, slots[k])
        copy.start()
        force_copies.append(copy)
    total = jnp.concatenate(piece(home), axis=0) - by_centre[0:3]
    inverse_mass = 1.0 / (1.0 + kind[...].astype(F32))
    velocity = vel[...]
    for copy in force_copies:
        copy.wait()
    arrived = force_in[leaders[0]]
    for k in leaders[1:]:
        arrived = arrived + force_in[k]
    total = total + jnp.concatenate(
        [arrived[:, m * atoms : (m + 1) * atoms] for m in range(3)], axis=0
    )
    forces = -total
    new_vel = velocity + TIME_STEP * forces * inverse_mass
    new_pos = here + TIME_STEP * new_vel
    state = jnp.concatenate([new_pos, new_vel, forces], axis=0)
    blocks = atoms // 128
    depth = float(atoms // 64)
    is_z = (lax.broadcasted_iota(jnp.int32, (9, 128), 0) == 2).astype(F32)

    def block_for(target):
        result = jnp.zeros((9, 128), F32)
        lift = (me[2] - target).astype(F32) * depth
        for b in range(blocks):
            mine = jnp.full((9, 128), owner_ref[b], jnp.int32) == target
            result = result + jnp.where(mine, state[:, 128 * b : 128 * b + 128] + is_z * lift, 0.0)
        return result

    move_copies = []
    for z in range(1, zs):
        target = lax.rem(me[2] + z, zs)
        move_out[z] = block_for(target)
        copy = push(z, move_out.at[z], move_in.at[z], move_send, move_recv, (0, 0, z))
        copy.start()
        move_copies.append(copy)
    out[me[2]] = block_for(me[2])
    for copy in move_copies:
        copy.wait()
    for z in range(1, zs):
        source = lax.rem(me[2] + zs - z, zs)
        out[source] = move_in[z]


def per_device(
    sizes,
    positions,
    velocities,
    species,
    pair_table,
    live_blocks,
    owners,
    radial_weight,
    center_embed,
    neighbour_embed,
    vector_weight,
    env_weight,
    vector_gate,
    latent_weight,
    energy_weight,
):
    atoms = positions.shape[4]
    count = pair_table.shape[4]
    width = latent_weight.shape[1]
    ch = vector_weight.shape[0]
    zs = sizes[2]
    smem = pl.BlockSpec(memory_space=pltpu.SMEM)
    vmem = pl.BlockSpec(memory_space=pltpu.VMEM)
    dma = pltpu.SemaphoreType.DMA
    result = pl.pallas_call(
        functools.partial(kernel, sizes),
        out_shape=jax.ShapeDtypeStruct((zs, 9, 128), F32),
        in_specs=[smem, smem] + [vmem] * 12,
        out_specs=vmem,
        scratch_shapes=weight_scratch(width, ch)
        + store_scratch(width, ch, count, atoms)
        + [
            pltpu.VMEM((atoms, count), BF16),
            pltpu.VMEM((atoms, count), BF16),
            pltpu.VMEM((1, 1, 3 * atoms), F32),
            pltpu.VMEM((SLOTS, 1, 3 * atoms), F32),
            pltpu.VMEM((SLOTS, 1, 3 * atoms), F32),
            pltpu.VMEM((SLOTS, 1, 3 * atoms), F32),
            pltpu.VMEM((zs, 9, 128), F32),
            pltpu.VMEM((zs, 9, 128), F32),
            dma((SLOTS,)),
            dma((SLOTS,)),
            dma((SLOTS,)),
            dma((SLOTS,)),
            dma((zs,)),
            dma((zs,)),
        ],
        compiler_params=pltpu.CompilerParams(
            collective_id=0, has_side_effects=True, vmem_limit_bytes=48 << 20
        ),
    )(
        live_blocks.reshape(1),
        owners.reshape(-1),
        positions.reshape(3, atoms),
        velocities.reshape(3, atoms),
        species.reshape(1, atoms),
        pair_table.reshape(3, count),
        radial_weight,
        center_embed,
        neighbour_embed,
        vector_weight,
        env_weight,
        vector_gate,
        latent_weight,
        energy_weight.reshape(1, width),
    )
    return result[None, None, None]


def solution(mesh):
    sizes = (mesh.shape["gx"], mesh.shape["gy"], mesh.shape["gz"])
    spread = ("gx", "gy", "gz")
    in_specs = (
        P(*spread, None, None),
        P(*spread, None, None),
        P(*spread, None),
        P(*spread, None, None),
        P(*spread),
        P(*spread, None),
    ) + (P(),) * 8
    return jax.shard_map(
        functools.partial(per_device, sizes),
        mesh=mesh,
        in_specs=in_specs,
        out_specs=P(*spread, None, None, None),
        check_vma=False,
    )
```

profile of v0, /device:TPU:0, one launch (start us, length us, event | category | flops | bytes accessed | tf_op | source)
XLA Modules:
  0.0 52.9 jit_solution(8282249537831900881)
XLA Ops:
  0.7 0.0 copy-start.11
  0.7 0.0 copy-start.10
  0.7 0.0 copy-start.7
  0.7 0.7 %copy-done.11 = f32[1,1,1,3,256]{4,2,3,1,0:T(1,128)S(1)} copy-done((f32[1,1,1,3,256]{4,2,3,1,0:T(1,128)S(1)}, f32[1,1,1,3,256]{4,2,3,1,0:T(1,128)}, u32[]{:S(2)}) %copy-start.11) | copy-done | bytes 3096
  1.3 0.0 copy-done.10
  1.4 0.0 copy-start.5
  1.4 0.0 copy-done.7
  1.4 0.1 copy.18.vector
  1.4 0.6 %copy-done.5 = s32[1,1,1,3,1536]{4,2,3,1,0:T(1,128)S(1)} copy-done((s32[1,1,1,3,1536]{4,2,3,1,0:T(1,128)S(1)}, s32[1,1,1,3,1536]{4,2,3,1,0:T(1,128)}, u32[]{:S(2)}) %copy-start.5) | copy-done | bytes 18456
  2.1 0.0 copy-start.6
  2.1 0.7 %copy-done.6 = f32[256,8]{0,1:T(8,128)S(1)} copy-done((f32[256,8]{0,1:T(8,128)S(1)}, f32[256,8]{0,1:T(8,128)}, u32[]{:S(2)}) %copy-start.6) | copy-done | bytes 8216
  2.8 0.0 copy-start.8
  2.8 0.1 copy.15.radial
  2.9 0.6 %copy-done.8 = f32[256,4]{0,1:T(4,128)S(1)} copy-done((f32[256,4]{0,1:T(4,128)S(1)}, f32[256,4]{0,1:T(4,128)}, u32[]{:S(2)}) %copy-start.8) | copy-done | bytes 4120
  3.5 0.0 copy-start.9
  3.5 0.1 copy.16.centre_e
  3.6 0.5 %copy-done.9 = f32[256,4]{0,1:T(4,128)S(1)} copy-done((f32[256,4]{0,1:T(4,128)S(1)}, f32[256,4]{0,1:T(4,128)}, u32[]{:S(2)}) %copy-start.9) | copy-done | bytes 4120
  4.1 0.1 copy.17.neigh_e
  4.3 0.0 copy-start
  4.3 0.0 copy-start.1
  4.3 0.0 copy-start.2
  4.3 0.0 copy-start.3
  4.3 0.0 copy-start.4
  4.3 1.4 %copy.19.latent_w = f32[2,256,288]{2,1,0:T(8,128)S(1)} copy(f32[2,256,288]{1,2,0:T(8,128)} %param.26) | data formatting | bytes 1179648 | tf_op args[12]
  5.7 0.0 copy-done
  5.7 0.0 copy-done.1
  5.7 0.0 copy-done.2
  5.8 0.0 copy-done.3
  5.8 0.0 copy-done.4
  5.8 46.5 %shard_map.136 = f32[2,9,128]{2,1,0:T(8,128)S(1)} custom-call(s32[1]{0:T(128)} %bitcast.12.live_ref, s32[2]{0:T(128)S(1)} %bitcast.17, f32[3,256]{1,0:T(4,128)S(1)} %get-tuple-element.6.pos, f32[3,256]{1,0:T(4,128)S(1)} %get-tuple-element.5.vel, s32[1,256]{1,0:T(1,128)S(1)} %bitcast.15, s32[3,1536]{1,0:T(4,128)S(1)} %bitcast.13, f32[256,8]{1,0:T(8,128)S(1)} %copy.15.radial, ...), custom_call_target="tpu_custom_call" | custom-call | tf_op jit(solution)/shard_map/pallas_call | solution.py:561
  52.3 0.6 %copy.20 = f32[1,1,1,2,9,128]{5,3,4,2,1,0:T(2,128)} copy(f32[1,1,1,2,9,128]{5,4,3,2,1,0:T(8,128)S(1)} %bitcast.14) | data formatting | bytes 18432 | tf_op jit(solution)/shard_map/broadcast_in_dim | solution.py:603
  (2 shorter events, 0.0 us)
Async XLA Ops:
  0.7 0.7 %copy-start.11 = (f32[1,1,1,3,256]{4,2,3,1,0:T(1,128)S(1)}, f32[1,1,1,3,256]{4,2,3,1,0:T(1,128)}, u32[]{:S(2)}) copy-start(f32[1,1,1,3,256]{4,2,3,1,0:T(1,128)} %param.14) | copy-start | bytes 9220
  0.7 0.7 %copy-start.10 = (f32[1,1,1,3,256]{4,2,3,1,0:T(1,128)S(1)}, f32[1,1,1,3,256]{4,2,3,1,0:T(1,128)}, u32[]{:S(2)}) copy-start(f32[1,1,1,3,256]{4,2,3,1,0:T(1,128)} %param.15) | copy-start | bytes 9220
  0.7 0.7 %copy-start.7 = (f32[32,8]{0,1:T(8,128)S(1)}, f32[32,8]{0,1:T(8,128)}, u32[]{:S(2)}) copy-start(f32[32,8]{0,1:T(8,128)} %param.23) | copy-start | bytes 3076
  1.4 0.7 %copy-start.5 = (s32[1,1,1,3,1536]{4,2,3,1,0:T(1,128)S(1)}, s32[1,1,1,3,1536]{4,2,3,1,0:T(1,128)}, u32[]{:S(2)}) copy-start(s32[1,1,1,3,1536]{4,2,3,1,0:T(1,128)} %param.17) | copy-start | bytes 55300
  2.1 0.7 %copy-start.6 = (f32[256,8]{0,1:T(8,128)S(1)}, f32[256,8]{0,1:T(8,128)}, u32[]{:S(2)}) copy-start(f32[256,8]{0,1:T(8,128)} %param.20) | copy-start | bytes 24580
  2.8 0.7 %copy-start.8 = (f32[256,4]{0,1:T(4,128)S(1)}, f32[256,4]{0,1:T(4,128)}, u32[]{:S(2)}) copy-start(f32[256,4]{0,1:T(4,128)} %param.21) | copy-start | bytes 12292
  3.5 0.7 %copy-start.9 = (f32[256,4]{0,1:T(4,128)S(1)}, f32[256,4]{0,1:T(4,128)}, u32[]{:S(2)}) copy-start(f32[256,4]{0,1:T(4,128)} %param.22) | copy-start | bytes 12292
  4.3 1.4 %copy-start = (f32[2,32,256]{2,1,0:T(8,128)S(1)}, f32[2,32,256]{2,1,0:T(8,128)}, u32[]{:S(2)}) copy-start(f32[2,32,256]{2,1,0:T(8,128)} %env_w.1) | copy-start | bytes 196612
  4.3 1.4 %copy-start.1 = (f32[32,256]{1,0:T(8,128)S(1)}, f32[32,256]{1,0:T(8,128)}, u32[]{:S(2)}) copy-start(f32[32,256]{1,0:T(8,128)} %gate_w.1) | copy-start | bytes 98308
  4.3 1.4 %copy-start.2 = (s32[1,1,1,256]{3,2,1,0:T(1,128)S(1)}, s32[1,1,1,256]{3,2,1,0:T(1,128)}, u32[]{:S(2)}) copy-start(s32[1,1,1,256]{3,2,1,0:T(1,128)} %param.16) | copy-start | bytes 3076
  4.3 1.4 %copy-start.3 = (f32[256]{0:T(256)S(1)}, f32[256]{0:T(256)}, u32[]{:S(2)}) copy-start(f32[256]{0:T(256)} %param.27) | copy-start | bytes 3076
  4.3 1.4 %copy-start.4 = (s32[1,1,1,2]{3,2,1,0:T(1,128)S(1)}, s32[1,1,1,2]{3,2,1,0:T(1,128)}, u32[]{:S(2)}) copy-start(s32[1,1,1,2]{3,2,1,0:T(1,128)} %param.19) | copy-start | bytes 28
where the time goes:
time: 53.2 us; the launch traced here: 52.9 us
  Pallas kernels  46.5 us (87%)
  local copies, waits for them, and re-layouts  5.58 us (10%)
  between operations  0.8 us (2%)
    pallas_call x1, Pallas kernels, per_device(): pl.pallas_call(functools.partial(kernel, sizes), out_shape=jax.ShapeDtype...  46.5 us
    unnamed x31, local copies, waits for them, and re-layouts  4.98 us

commit v1 on v0

--- a/solution.py
+++ b/solution.py
@@ -10,7 +10,7 @@
 CUTOFF = 5.0
 ENV_SCALE = 0.4
 TIME_STEP = 0.2
-CHUNK = 256
+CHUNK = 512
 SLOTS = 27
 F32 = jnp.float32
 BF16 = jnp.bfloat16
@@ -86,12 +86,12 @@
 def prepare(weights, scratch):
     radial, centre_e, neigh_e, vector, env_w, gate_w, latent_w, energy = weights
     (w_first, wa_h, wa_l, wb_h, wb_l, s0, s1, t0_h, t0_l, t1_h, t1_l, gate_t, e0_t, e1_t, back_h, back_l, ew) = scratch
-    width = radial.shape[0]
-    channels = vector.shape[0]
-    radial_t = wide(radial[...], 128).T[:8]
-    centre_t = wide(centre_e[...], 128).T[:8]
-    neigh_t = wide(neigh_e[...], 128).T[:8]
-    vector_t = wide(tall(vector[...], 128), 128).T[:8, :channels]
+    width = radial.shape[1]
+    channels = vector.shape[1]
+    radial_t = radial[...]
+    centre_t = tall(centre_e[...], 8)
+    neigh_t = tall(neigh_e[...], 8)
+    vector_t = vector[...]
     zeros = jnp.zeros((8, 128), F32)
     vector_tp = wide(vector_t, 128)
     first_t = jnp.concatenate(
@@ -103,16 +103,15 @@
         axis=0,
     )
     w_first[...] = pack3(first_t)
-    layer0 = wide(latent_w[0], 384).T
-    layer1 = wide(latent_w[1], 384).T
-    high, low = split(jnp.concatenate([latent_w[0][:, :width], gate_w[...], env_w[0]], axis=0))
+    layer0, layer1 = latent_w[0], latent_w[1]
+    high, low = split(jnp.concatenate([layer0[:width].T, gate_w[...], env_w[0]], axis=0))
     wa_h[...], wa_l[...] = high, low
-    high, low = split(jnp.concatenate([latent_w[1][:, :width], env_w[1]], axis=0))
+    high, low = split(jnp.concatenate([layer1[:width].T, env_w[1]], axis=0))
     wb_h[...], wb_l[...] = high, low
     s0[...] = pack3(layer0[width : width + channels])
     s1[...] = pack3(layer1[width : width + channels])
-    t0_h[...], t0_l[...] = split(layer0[: width + channels])
-    t1_h[...], t1_l[...] = split(layer1[: width + channels])
+    t0_h[...], t0_l[...] = split(layer0)
+    t1_h[...], t1_l[...] = split(layer1)
     gate_t[...] = pack3(gate_w[...])
     e0_t[...] = pack3(env_w[0])
     e1_t[...] = pack3(env_w[1])
@@ -122,13 +121,13 @@
 
 
 def hot_matrices(pair, mem_t, nbr_t, atoms):
-    count = pair.shape[1]
+    count = pair.shape[2]
     labels = lax.broadcasted_iota(jnp.int32, (atoms, CHUNK), 0)
 
     def chunk(i, carry):
         here = pl.ds(pl.multiple_of(i * CHUNK, CHUNK), CHUNK)
-        centre = pair[0:1, here]
-        atom = pair[1:2, here] & (atoms - 1)
+        centre = pair[0, :, here]
+        atom = pair[1, :, here] & (atoms - 1)
         mem_t[:, here] = (labels == centre).astype(F32).astype(BF16)
         nbr_t[:, here] = (labels == atom).astype(F32).astype(BF16)
         return carry
@@ -162,19 +161,15 @@
     )
 
 
-def gradient(table, near_table, pair, live, weights, hots, store):
+def gradient(table, near, pair, live, weights, hots, store):
     (w_first, wa_h, wa_l, wb_h, wb_l, s0, s1, t0_h, t0_l, t1_h, t1_l, gate_t, e0_t, e1_t, back_h, back_l, ew) = weights
     mem_t, nbr_t = hots
-    (geo, trig, silu0, dsilu0, upper, lower, silu1, dsilu1, small, at0s, v1s, dv1s, dlat, acc, spread_acc) = store
+    (geo, trig, silu0, dsilu0, upper, lower, silu1, dsilu1, small, at0s, v1s, dv1s, dlat, acc, firsts, d_bases) = store
     atoms, count = mem_t.shape
     depth = float(atoms // 64)
     width = silu0.shape[0]
     ch = v1s.shape[0] // 3
     steps = count // CHUNK
-    slot_rows = lax.broadcasted_iota(jnp.int32, (32, CHUNK), 0)
-    lanes = lax.broadcasted_iota(jnp.int32, (1, CHUNK), 1)
-    orders = (lax.broadcasted_iota(jnp.int32, (8, CHUNK), 0) + 1).astype(F32)
-    kinds = lax.broadcasted_iota(jnp.int32, (8, CHUNK), 0)
     vw, vb, g0, ep0, ep1, dvw = (slice(k * ch, (k + 1) * ch) for k in range(6))
 
     def at(i):
@@ -201,41 +196,35 @@
         value = ew[...]
         return jnp.concatenate([value] * (CHUNK // 128), axis=1)
 
+    slot = pair[1] // atoms
+    hot = lax.broadcasted_iota(jnp.int32, (32, count), 0) == slot
+    far = dot(table, nbr_t[...])
+    far = far[:96] + far[96:192] + far[192:]
+    picks = [jnp.sum(jnp.where(hot, far[32 * m : 32 * m + 32], 0.0), axis=0, keepdims=True) for m in range(3)]
+    dx = picks[0] + (slot // 9 - 1).astype(F32) * 8.0 - near[0:1]
+    dy = picks[1] + (slot // 3 % 3 - 1).astype(F32) * 8.0 - near[1:2]
+    dz = picks[2] + (slot % 3 - 1).astype(F32) * depth - near[2:3]
+    distance = jnp.sqrt(dx * dx + dy * dy + dz * dz)
+    inverse = 1.0 / distance
+    ratio = distance / CUTOFF
+    lanes = lax.broadcasted_iota(jnp.int32, (1, count), 1)
+    use = (lanes < live * 128).astype(F32)
+    bump = 1.0 - ratio * ratio
+    geo[0:3] = jnp.concatenate([dx, dy, dz], axis=0) * inverse
+    geo[3:4] = bump * bump * use
+    geo[4:5] = inverse
+    geo[5:6] = bump * use * (-4.0 / CUTOFF) * ratio
+    orders = (lax.broadcasted_iota(jnp.int32, (8, count), 0) + 1).astype(F32)
+    angle = orders * jnp.pi * distance / CUTOFF
+    norm = (2.0 / CUTOFF) ** 0.5 * inverse
+    basis = norm * jnp.sin(angle)
+    trig[...] = norm * (orders * (jnp.pi / CUTOFF)) * jnp.cos(angle) - basis * inverse
+    other_hot = (lax.broadcasted_iota(jnp.int32, (8, count), 0) == pair[2]).astype(F32)
+    firsts[...] = stack3(jnp.concatenate([basis, near[8:16], other_hot], axis=0))
+
     def phase_a(here, i):
-        slot = pair[1:2, here] // atoms
-        far = dot(table, nbr_t[:, here])
-        far = far[:96] + far[96:192] + far[192:]
-        hot = slot_rows == slot
-        picks = [
-            jnp.sum(jnp.where(hot, far[32 * m : 32 * m + 32], 0.0), axis=0, keepdims=True) for m in range(3)
-        ]
-        near = dot(near_table, mem_t[:, here])
-        centre_hot = near[24:32]
-        near = near[0:8] + near[8:16] + near[16:24]
-        shift_x = (slot // 9 - 1).astype(F32) * 8.0
-        shift_y = (slot // 3 % 3 - 1).astype(F32) * 8.0
-        shift_z = (slot % 3 - 1).astype(F32) * depth
-        dx = picks[0] + shift_x - near[0:1]
-        dy = picks[1] + shift_y - near[1:2]
-        dz = picks[2] + shift_z - near[2:3]
-        distance = jnp.sqrt(dx * dx + dy * dy + dz * dz)
-        inverse = 1.0 / distance
-        unit = jnp.concatenate([dx, dy, dz], axis=0) * inverse
-        ratio = distance / CUTOFF
-        use = (i * CHUNK + lanes < live * 128).astype(F32)
-        bump = 1.0 - ratio * ratio
-        envelope = bump * bump * use
-        slope = bump * use * (-4.0 / CUTOFF) * ratio
-        angle = orders * jnp.pi * distance / CUTOFF
-        norm = (2.0 / CUTOFF) ** 0.5 * inverse
-        basis = norm * jnp.sin(angle)
-        trig[:, here] = norm * (orders * (jnp.pi / CUTOFF)) * jnp.cos(angle) - basis * inverse
-        geo[0:3, here] = unit
-        geo[3:4, here] = envelope
-        geo[4:5, here] = inverse
-        geo[5:6, here] = slope
-        other_hot = (kinds == pair[2:3, here]).astype(F32)
-        first = dot(w_first[...], stack3(jnp.concatenate([basis, centre_hot, other_hot], axis=0)))
+        unit, envelope = geo[0:3, here], geo[3:4, here]
+        first = dot(w_first[...], firsts[:, here])
         value, deriv = silu_pair(first[:width])
         silu0[:, here] = value
         dsilu0[:, here] = deriv
@@ -303,7 +292,6 @@
         scatter(dv1 * tile3(small[g0, here]) + times3(unit, d_scalar * vw_here), here)
 
     denv0 = loop(phase_d)
-    spread_acc[...] = jnp.zeros_like(spread_acc)
 
     def phase_e(here, i):
         unit, envelope = geo[0:3, here], geo[3:4, here]
@@ -319,22 +307,22 @@
         d_first = jnp.concatenate(
             [d_latent * envelope * dsilu0[:, here], tall(envelope * d_vw, 128)], axis=0
         )
-        d_basis = mul3(back_h[...], back_l[...], d_first)[:8]
-        d_distance = jnp.sum(d_basis * trig[:, here], axis=0, keepdims=True) + d_envelope * geo[5:6, here]
-        along = jnp.sum(unit * d_unit, axis=0, keepdims=True)
-        d_move = unit * d_distance + (d_unit - unit * along) * geo[4:5, here]
-        hot = slot_rows == pair[1:2, here] // atoms
-        high, low = split(
-            jnp.concatenate([jnp.where(hot, d_move[m : m + 1], 0.0) for m in range(3)], axis=0)
-        )
-        spread_acc[0:192] += dot_t(jnp.concatenate([high, low], axis=0), nbr_t[:, here])
-        high, low = split(tall(d_move, 16))
-        spread_acc[192:224] += dot_t(jnp.concatenate([high, low], axis=0), mem_t[:, here])
+        d_bases[0:8, here] = mul3(back_h[...], back_l[...], d_first)[:8]
+        geo[6:7, here] = d_envelope
+        geo[8:11, here] = d_unit
 
     lax.fori_loop(0, steps, lambda i, c: (phase_e(at(i), i), c)[1], 0)
-    by_slot = spread_acc[0:96] + spread_acc[96:192]
-    by_centre = spread_acc[192:208] + spread_acc[208:224]
-    return by_slot, by_centre
+    unit, d_unit = geo[0:3], geo[8:11]
+    d_distance = jnp.sum(d_bases[...] * trig[...], axis=0, keepdims=True) + geo[6:7] * geo[5:6]
+    along = jnp.sum(unit * d_unit, axis=0, keepdims=True)
+    d_move = unit * d_distance + (d_unit - unit * along) * geo[4:5]
+    high, low = split(tall(d_move, 16))
+    by_centre = dot_t(jnp.concatenate([high, low], axis=0), mem_t[...])
+    high, low = split(
+        jnp.concatenate([jnp.where(hot, d_move[m : m + 1], 0.0) for m in range(3)], axis=0)
+    )
+    by_slot = dot_t(jnp.concatenate([high, low], axis=0), nbr_t[...])
+    return by_slot[:96] + by_slot[96:], by_centre[:16] + by_centre[16:]
 
 
 def weight_scratch(width, ch):
@@ -381,7 +369,8 @@
         f(3 * ch, count),
         f(width, count),
         f(6 * ch, atoms),
-        f(224, atoms),
+        pltpu.VMEM((128, count), BF16),
+        f(8, count),
     ]
 
 
@@ -409,11 +398,19 @@
     *scratch,
 ):
     xs, ys, zs = sizes
-    weights = (radial, centre_e, neigh_e, vector, env_w, gate_w, latent_w, energy)
-    w_scratch, store = scratch[:17], scratch[17:32]
-    (mem_t, nbr_t, own, halo, force_out, force_in, move_out, move_in,
-     pos_send, pos_recv, force_send, force_recv, move_send, move_recv) = scratch[32:]
-    atoms = pos.shape[1]
+    weights = scratch[47:]
+    w_scratch, store = scratch[:17], scratch[17:33]
+    (mem_t, nbr_t, halo, force_out, force_in, move_out, move_in,
+     pos_send, pos_recv, force_send, force_recv, move_send, move_recv, load_sem) = scratch[33:47]
+    loads = [
+        pltpu.make_async_copy(source, target, load_sem.at[k])
+        for k, (source, target) in enumerate(
+            zip((radial, centre_e, neigh_e, vector, env_w, gate_w, latent_w, energy), weights)
+        )
+    ]
+    for load in loads:
+        load.start()
+    atoms = vel.shape[2]
     me = (lax.axis_index("gx"), lax.axis_index("gy"), lax.axis_index("gz"))
 
     def device(step):
@@ -434,9 +431,7 @@
     barrier = pltpu.get_barrier_semaphore()
     for step in partners:
         pl.semaphore_signal(barrier, inc=1, device_id=device(step), device_id_type=MESH)
-    here = pos[...]
-    for m in range(3):
-        own[0, :, m * atoms : (m + 1) * atoms] = here[m : m + 1]
+    here = jnp.concatenate([pos[0, :, m * atoms : (m + 1) * atoms] for m in range(3)], axis=0)
     pl.semaphore_wait(barrier, len(partners))
 
     def push(k, source, target, send, recv, step):
@@ -446,18 +441,21 @@
         )
 
     pos_copies = [
-        push(k, own.at[0], halo.at[k], pos_send, pos_recv, tuple(-v for v in slots[k])) for k in leaders
+        push(k, pos.at[0], halo.at[k], pos_send, pos_recv, tuple(-v for v in slots[k])) for k in leaders
     ]
     for copy in pos_copies:
         copy.start()
 
-    prepare(weights, w_scratch)
     hot_matrices(pair, mem_t, nbr_t, atoms)
     species_hot = (
         lax.broadcasted_iota(jnp.int32, (8, atoms), 0) == kind[...]
     ).astype(F32)
     high, mid, low = (v.astype(F32) for v in split3(tall(here, 8)))
-    near_table = jnp.concatenate([high, mid, low, species_hot], axis=0).astype(BF16)
+    near = dot(jnp.concatenate([high, mid, low, species_hot], axis=0).astype(BF16), mem_t[...])
+    near = jnp.concatenate([near[0:8] + near[8:16] + near[16:24], near[24:32]], axis=0)
+    for load in loads:
+        load.wait()
+    prepare(weights, w_scratch)
 
     for copy in pos_copies:
         copy.wait()
@@ -465,12 +463,12 @@
     for m in range(3):
         cut = slice(m * atoms, (m + 1) * atoms)
         for k in range(SLOTS):
-            rows.append(own[0, :, cut] if leader[k] == home else halo[leader[k], :, cut])
+            rows.append(pos[0, :, cut] if leader[k] == home else halo[leader[k], :, cut])
         rows.append(jnp.zeros((32 - SLOTS, atoms), F32))
     table = jnp.concatenate(split3(jnp.concatenate(rows, axis=0)), axis=0)
 
     by_slot, by_centre = gradient(
-        table, near_table, pair, live_ref[0], w_scratch, (mem_t, nbr_t), store
+        table, near, pair, live_ref[0], w_scratch, (mem_t, nbr_t), store
     )
 
     members = {k: [j for j in range(SLOTS) if leader[j] == k] for k in leaders + [home]}
@@ -493,7 +491,7 @@
         force_copies.append(copy)
     total = jnp.concatenate(piece(home), axis=0) - by_centre[0:3]
     inverse_mass = 1.0 / (1.0 + kind[...].astype(F32))
-    velocity = vel[...]
+    velocity = jnp.concatenate([vel[0], vel[1], vel[2]], axis=0)
     for copy in force_copies:
         copy.wait()
     arrived = force_in[leaders[0]]
@@ -558,17 +556,26 @@
     smem = pl.BlockSpec(memory_space=pltpu.SMEM)
     vmem = pl.BlockSpec(memory_space=pltpu.VMEM)
     dma = pltpu.SemaphoreType.DMA
+    weights = (
+        radial_weight.T,
+        center_embed.T,
+        neighbour_embed.T,
+        vector_weight.T,
+        env_weight,
+        vector_gate,
+        jnp.swapaxes(latent_weight, 1, 2),
+        energy_weight.reshape(1, width),
+    )
     result = pl.pallas_call(
         functools.partial(kernel, sizes),
         out_shape=jax.ShapeDtypeStruct((zs, 9, 128), F32),
-        in_specs=[smem, smem] + [vmem] * 12,
+        in_specs=[smem, smem] + [vmem] * 4 + [pl.BlockSpec(memory_space=pl.ANY)] * 8,
         out_specs=vmem,
         scratch_shapes=weight_scratch(width, ch)
         + store_scratch(width, ch, count, atoms)
         + [
             pltpu.VMEM((atoms, count), BF16),
             pltpu.VMEM((atoms, count), BF16),
-            pltpu.VMEM((1, 1, 3 * atoms), F32),
             pltpu.VMEM((SLOTS, 1, 3 * atoms), F32),
             pltpu.VMEM((SLOTS, 1, 3 * atoms), F32),
             pltpu.VMEM((SLOTS, 1, 3 * atoms), F32),
@@ -580,25 +587,20 @@
             dma((SLOTS,)),
             dma((zs,)),
             dma((zs,)),
-        ],
+            dma((8,)),
+        ]
+        + [pltpu.VMEM(w.shape, F32) for w in weights],
         compiler_params=pltpu.CompilerParams(
             collective_id=0, has_side_effects=True, vmem_limit_bytes=48 << 20
         ),
     )(
         live_blocks.reshape(1),
         owners.reshape(-1),
-        positions.reshape(3, atoms),
-        velocities.reshape(3, atoms),
+        positions.reshape(1, 1, 3 * atoms),
+        velocities.reshape(3, 1, atoms),
         species.reshape(1, atoms),
-        pair_table.reshape(3, count),
-        radial_weight,
-        center_embed,
-        neighbour_embed,
-        vector_weight,
-        env_weight,
-        vector_gate,
-        latent_weight,
-        energy_weight.reshape(1, width),
+        pair_table.reshape(3, 1, count),
+        *weights,
     )
     return result[None, None, None]
 

time: 53.2 us -> 44.5 us (0.84)
  Pallas kernels: 46.5 us -> 35.9 us
  local copies, waits for them, and re-layouts: 5.58 us -> 7.38 us
    pallas_call x1, Pallas kernels: 46.5 us -> 35.9 us  [per_device(): pl.pallas_call(functools.partial(kernel, sizes), out_shape=jax.ShapeDtype...]
    unnamed x31 -> x26, local copies, waits for them, and re-layouts: 4.98 us -> 6.78 us
where the time goes in v1:
time: 44.5 us; the launch traced here: 44 us
  Pallas kernels  35.9 us (81%)
  local copies, waits for them, and re-layouts  7.38 us (17%)
  between operations  0.71 us (2%)
    pallas_call x1, Pallas kernels, per_device(): pl.pallas_call(functools.partial(kernel, sizes), out_shape=jax.ShapeDtype...  35.9 us
    unnamed x26, local copies, waits for them, and re-layouts  6.78 us

profile of v1, /device:TPU:0, one launch (start us, length us, event | category | flops | bytes accessed | tf_op | source)
XLA Modules:
  0.0 44.0 jit_solution(15870251220000047208)
XLA Ops:
  0.0 0.0 copy-start.3
  0.7 0.0 copy-start.5
  0.7 0.0 copy-start.11
  0.7 0.0 copy-start.10
  0.7 0.0 copy-start.12
  0.7 0.0 copy-done.3
  0.7 0.6 %copy-done.5 = f32[256,4]{0,1:T(4,128)S(1)} copy-done((f32[256,4]{0,1:T(4,128)S(1)}, f32[256,4]{0,1:T(4,128)}, u32[]{:S(2)}) %copy-start.5) | copy-done | bytes 4120
  1.4 0.0 copy-done.11
  1.4 0.0 copy-done.10
  1.4 0.0 copy-done.12
  1.4 0.0 copy-start
  1.4 1.1 %copy-done = f32[2,256,288]{1,2,0:T(8,128)S(1)} copy-done((f32[2,256,288]{1,2,0:T(8,128)S(1)}, f32[2,256,288]{1,2,0:T(8,128)}, u32[]{:S(2)}) %copy-start) | copy-done | bytes 589848
  2.4 0.0 copy-start.1
  2.4 0.8 %copy-done.1 = f32[2,32,256]{2,1,0:T(8,128)S(1)} copy-done((f32[2,32,256]{2,1,0:T(8,128)S(1)}, f32[2,32,256]{2,1,0:T(8,128)}, u32[]{:S(2)}) %copy-start.1) | copy-done | bytes 65560
  3.3 0.0 copy-start.2
  3.3 0.8 %copy-done.2 = f32[32,256]{1,0:T(8,128)S(1)} copy-done((f32[32,256]{1,0:T(8,128)S(1)}, f32[32,256]{1,0:T(8,128)}, u32[]{:S(2)}) %copy-start.2) | copy-done | bytes 32792
  4.0 0.0 copy-start.4
  4.0 0.7 %copy-done.4 = f32[256,8]{0,1:T(8,128)S(1)} copy-done((f32[256,8]{0,1:T(8,128)S(1)}, f32[256,8]{0,1:T(8,128)}, u32[]{:S(2)}) %copy-start.4) | copy-done | bytes 8216
  4.7 0.0 copy-start.6
  4.7 0.7 %copy-done.6 = f32[256,4]{0,1:T(4,128)S(1)} copy-done((f32[256,4]{0,1:T(4,128)S(1)}, f32[256,4]{0,1:T(4,128)}, u32[]{:S(2)}) %copy-start.6) | copy-done | bytes 4120
  5.4 0.0 copy-start.7
  5.4 0.7 %copy-done.7 = f32[32,8]{0,1:T(8,128)S(1)} copy-done((f32[32,8]{0,1:T(8,128)S(1)}, f32[32,8]{0,1:T(8,128)}, u32[]{:S(2)}) %copy-start.7) | copy-done | bytes 1048
  6.1 0.0 copy-start.8
  6.1 0.7 %copy-done.8 = f32[1,1,1,3,256]{4,2,3,1,0:T(1,128)S(1)} copy-done((f32[1,1,1,3,256]{4,2,3,1,0:T(1,128)S(1)}, f32[1,1,1,3,256]{4,2,3,1,0:T(1,128)}, u32[]{:S(2)}) %copy-start.8) | copy-done | bytes 3096
  6.8 0.0 copy-start.9
  6.8 0.7 %copy-done.9 = f32[1,1,1,3,256]{4,2,3,1,0:T(1,128)S(1)} copy-done((f32[1,1,1,3,256]{4,2,3,1,0:T(1,128)S(1)}, f32[1,1,1,3,256]{4,2,3,1,0:T(1,128)}, u32[]{:S(2)}) %copy-start.9) | copy-done | bytes 3096
  7.5 35.9 %shard_map.136 = f32[2,9,128]{2,1,0:T(8,128)S(1)} custom-call(s32[1]{0:T(128)} %bitcast.13.live_ref, s32[2]{0:T(128)S(1)} %bitcast.25, f32[1,1,768]{2,1,0:T(1,128)S(1)} %bitcast.21, f32[3,1,256]{2,1,0:T(1,128)S(1)} %bitcast.22, s32[1,256]{1,0:T(1,128)S(1)} %bitcast.23, s32[3,1,1536]{2,1,0:T(1,128)S(1)} %bitcast.16, f32[8,256]{1,0:T(8,128)S(1)} %bitcast.17, ...), custom_call_target="tpu_custom_call" | custom-call | tf_op jit(solution)/shard_map/pallas_call | solution.py:569
  43.4 0.6 %copy.15 = f32[1,1,1,2,9,128]{5,3,4,2,1,0:T(2,128)} copy(f32[1,1,1,2,9,128]{5,4,3,2,1,0:T(8,128)S(1)} %bitcast.15) | data formatting | bytes 18432 | tf_op jit(solution)/shard_map/broadcast_in_dim | solution.py:605
Async XLA Ops:
  0.0 0.7 %copy-start.3 = (s32[1,1,1,3,1536]{4,2,3,1,0:T(1,128)S(1)}, s32[1,1,1,3,1536]{4,2,3,1,0:T(1,128)}, u32[]{:S(2)}) copy-start(s32[1,1,1,3,1536]{4,2,3,1,0:T(1,128)} %param.17) | copy-start | bytes 55300
  0.7 0.7 %copy-start.5 = (f32[256,4]{0,1:T(4,128)S(1)}, f32[256,4]{0,1:T(4,128)}, u32[]{:S(2)}) copy-start(f32[256,4]{0,1:T(4,128)} %param.21) | copy-start | bytes 12292
  0.7 0.7 %copy-start.11 = (f32[256]{0:T(256)S(1)}, f32[256]{0:T(256)}, u32[]{:S(2)}) copy-start(f32[256]{0:T(256)} %param.27) | copy-start | bytes 3076
  0.7 0.7 %copy-start.10 = (s32[1,1,1,256]{3,2,1,0:T(1,128)S(1)}, s32[1,1,1,256]{3,2,1,0:T(1,128)}, u32[]{:S(2)}) copy-start(s32[1,1,1,256]{3,2,1,0:T(1,128)} %param.16) | copy-start | bytes 3076
  0.7 0.7 %copy-start.12 = (s32[1,1,1,2]{3,2,1,0:T(1,128)S(1)}, s32[1,1,1,2]{3,2,1,0:T(1,128)}, u32[]{:S(2)}) copy-start(s32[1,1,1,2]{3,2,1,0:T(1,128)} %param.19) | copy-start | bytes 28
  1.4 1.1 %copy-start = (f32[2,256,288]{1,2,0:T(8,128)S(1)}, f32[2,256,288]{1,2,0:T(8,128)}, u32[]{:S(2)}) copy-start(f32[2,256,288]{1,2,0:T(8,128)} %param.26) | copy-start | bytes 1769476
  2.4 0.8 %copy-start.1 = (f32[2,32,256]{2,1,0:T(8,128)S(1)}, f32[2,32,256]{2,1,0:T(8,128)}, u32[]{:S(2)}) copy-start(f32[2,32,256]{2,1,0:T(8,128)} %env_w.1) | copy-start | bytes 196612
  3.3 0.8 %copy-start.2 = (f32[32,256]{1,0:T(8,128)S(1)}, f32[32,256]{1,0:T(8,128)}, u32[]{:S(2)}) copy-start(f32[32,256]{1,0:T(8,128)} %gate_w.1) | copy-start | bytes 98308
  4.0 0.7 %copy-start.4 = (f32[256,8]{0,1:T(8,128)S(1)}, f32[256,8]{0,1:T(8,128)}, u32[]{:S(2)}) copy-start(f32[256,8]{0,1:T(8,128)} %param.20) | copy-start | bytes 24580
  4.7 0.7 %copy-start.6 = (f32[256,4]{0,1:T(4,128)S(1)}, f32[256,4]{0,1:T(4,128)}, u32[]{:S(2)}) copy-start(f32[256,4]{0,1:T(4,128)} %param.22) | copy-start | bytes 12292
  5.4 0.7 %copy-start.7 = (f32[32,8]{0,1:T(8,128)S(1)}, f32[32,8]{0,1:T(8,128)}, u32[]{:S(2)}) copy-start(f32[32,8]{0,1:T(8,128)} %param.23) | copy-start | bytes 3076
  6.1 0.7 %copy-start.8 = (f32[1,1,1,3,256]{4,2,3,1,0:T(1,128)S(1)}, f32[1,1,1,3,256]{4,2,3,1,0:T(1,128)}, u32[]{:S(2)}) copy-start(f32[1,1,1,3,256]{4,2,3,1,0:T(1,128)} %param.14) | copy-start | bytes 9220
  6.8 0.7 %copy-start.9 = (f32[1,1,1,3,256]{4,2,3,1,0:T(1,128)S(1)}, f32[1,1,1,3,256]{4,2,3,1,0:T(1,128)}, u32[]{:S(2)}) copy-start(f32[1,1,1,3,256]{4,2,3,1,0:T(1,128)} %param.15) | copy-start | bytes 9220

commit v2 on v1

--- a/solution.py
+++ b/solution.py
@@ -10,7 +10,7 @@
 CUTOFF = 5.0
 ENV_SCALE = 0.4
 TIME_STEP = 0.2
-CHUNK = 512
+CHUNK = 768
 SLOTS = 27
 F32 = jnp.float32
 BF16 = jnp.bfloat16
@@ -380,33 +380,19 @@
 
 def kernel(
     sizes,
-    live_ref,
-    owner_ref,
-    pos,
-    vel,
-    kind,
-    pair,
-    radial,
-    centre_e,
-    neigh_e,
-    vector,
-    env_w,
-    gate_w,
-    latent_w,
-    energy,
-    out,
-    *scratch,
+    *refs,
 ):
     xs, ys, zs = sizes
-    weights = scratch[47:]
+    sources, out, scratch = refs[:14], refs[14], refs[15:]
+    loaded = scratch[47:]
+    pair, kind, pos, live_ref, vel, owner_ref = loaded[:6]
+    weights = loaded[6:]
     w_scratch, store = scratch[:17], scratch[17:33]
     (mem_t, nbr_t, halo, force_out, force_in, move_out, move_in,
      pos_send, pos_recv, force_send, force_recv, move_send, move_recv, load_sem) = scratch[33:47]
     loads = [
         pltpu.make_async_copy(source, target, load_sem.at[k])
-        for k, (source, target) in enumerate(
-            zip((radial, centre_e, neigh_e, vector, env_w, gate_w, latent_w, energy), weights)
-        )
+        for k, (source, target) in enumerate(zip(sources, loaded))
     ]
     for load in loads:
         load.start()
@@ -431,7 +417,6 @@
     barrier = pltpu.get_barrier_semaphore()
     for step in partners:
         pl.semaphore_signal(barrier, inc=1, device_id=device(step), device_id_type=MESH)
-    here = jnp.concatenate([pos[0, :, m * atoms : (m + 1) * atoms] for m in range(3)], axis=0)
     pl.semaphore_wait(barrier, len(partners))
 
     def push(k, source, target, send, recv, step):
@@ -441,19 +426,22 @@
         )
 
     pos_copies = [
-        push(k, pos.at[0], halo.at[k], pos_send, pos_recv, tuple(-v for v in slots[k])) for k in leaders
+        push(k, sources[2].at[0], halo.at[k], pos_send, pos_recv, tuple(-v for v in slots[k])) for k in leaders
     ]
     for copy in pos_copies:
         copy.start()
 
+    for load in loads[:3]:
+        load.wait()
     hot_matrices(pair, mem_t, nbr_t, atoms)
+    here = jnp.concatenate([pos[0, :, m * atoms : (m + 1) * atoms] for m in range(3)], axis=0)
     species_hot = (
         lax.broadcasted_iota(jnp.int32, (8, atoms), 0) == kind[...]
     ).astype(F32)
     high, mid, low = (v.astype(F32) for v in split3(tall(here, 8)))
     near = dot(jnp.concatenate([high, mid, low, species_hot], axis=0).astype(BF16), mem_t[...])
     near = jnp.concatenate([near[0:8] + near[8:16] + near[16:24], near[24:32]], axis=0)
-    for load in loads:
+    for load in loads[3:]:
         load.wait()
     prepare(weights, w_scratch)
 
@@ -468,7 +456,7 @@
     table = jnp.concatenate(split3(jnp.concatenate(rows, axis=0)), axis=0)
 
     by_slot, by_centre = gradient(
-        table, near, pair, live_ref[0], w_scratch, (mem_t, nbr_t), store
+        table, near, pair, live_ref[...], w_scratch, (mem_t, nbr_t), store
     )
 
     members = {k: [j for j in range(SLOTS) if leader[j] == k] for k in leaders + [home]}
@@ -512,7 +500,7 @@
         result = jnp.zeros((9, 128), F32)
         lift = (me[2] - target).astype(F32) * depth
         for b in range(blocks):
-            mine = jnp.full((9, 128), owner_ref[b], jnp.int32) == target
+            mine = jnp.broadcast_to(owner_ref[:, b : b + 1], (9, 128)) == target
             result = result + jnp.where(mine, state[:, 128 * b : 128 * b + 128] + is_z * lift, 0.0)
         return result
 
@@ -553,10 +541,14 @@
     width = latent_weight.shape[1]
     ch = vector_weight.shape[0]
     zs = sizes[2]
-    smem = pl.BlockSpec(memory_space=pltpu.SMEM)
-    vmem = pl.BlockSpec(memory_space=pltpu.VMEM)
     dma = pltpu.SemaphoreType.DMA
-    weights = (
+    operands = (
+        pair_table.reshape(3, 1, count),
+        species.reshape(1, atoms),
+        positions.reshape(1, 1, 3 * atoms),
+        live_blocks.reshape(1, 1),
+        velocities.reshape(3, 1, atoms),
+        owners.reshape(1, -1),
         radial_weight.T,
         center_embed.T,
         neighbour_embed.T,
@@ -569,8 +561,8 @@
     result = pl.pallas_call(
         functools.partial(kernel, sizes),
         out_shape=jax.ShapeDtypeStruct((zs, 9, 128), F32),
-        in_specs=[smem, smem] + [vmem] * 4 + [pl.BlockSpec(memory_space=pl.ANY)] * 8,
-        out_specs=vmem,
+        in_specs=[pl.BlockSpec(memory_space=pl.ANY)] * 14,
+        out_specs=pl.BlockSpec(memory_space=pltpu.VMEM),
         scratch_shapes=weight_scratch(width, ch)
         + store_scratch(width, ch, count, atoms)
         + [
@@ -587,21 +579,13 @@
             dma((SLOTS,)),
             dma((zs,)),
             dma((zs,)),
-            dma((8,)),
+            dma((14,)),
         ]
-        + [pltpu.VMEM(w.shape, F32) for w in weights],
+        + [pltpu.VMEM(v.shape, v.dtype) for v in operands],
         compiler_params=pltpu.CompilerParams(
-            collective_id=0, has_side_effects=True, vmem_limit_bytes=48 << 20
+            collective_id=0, has_side_effects=True, vmem_limit_bytes=60 << 20
         ),
-    )(
-        live_blocks.reshape(1),
-        owners.reshape(-1),
-        positions.reshape(1, 1, 3 * atoms),
-        velocities.reshape(3, 1, atoms),
-        species.reshape(1, atoms),
-        pair_table.reshape(3, 1, count),
-        *weights,
-    )
+    )(*operands)
     return result[None, None, None]
 
 

time: 44.5 us -> 36.3 us (0.82)
  local copies, waits for them, and re-layouts: 7.38 us -> 1.32 us
  Pallas kernels: 35.9 us -> 34.1 us
    unnamed x26 -> x0, local copies, waits for them, and re-layouts: 6.78 us -> none
    pallas_call x1, Pallas kernels: 35.9 us -> 34.1 us  [per_device(): pl.pallas_call(functools.partial(kernel, sizes), out_shape=jax.ShapeDtype...]
    broadcast_in_dim x1, local copies, waits for them, and re-layouts: 0.6 us -> 1.32 us  [per_device(): return result[None, None, None]]
where the time goes in v2:
time: 36.3 us; the launch traced here: 36.1 us
  Pallas kernels  34.1 us (94%)
  local copies, waits for them, and re-layouts  1.32 us (4%)
  between operations  0.66 us (2%)
    pallas_call x1, Pallas kernels, per_device(): pl.pallas_call(functools.partial(kernel, sizes), out_shape=jax.ShapeDtype...  34.1 us
    broadcast_in_dim x1, local copies, waits for them, and re-layouts, per_device(): return result[None, None, None]  1.32 us

profile of v2, /device:TPU:0, one launch (start us, length us, event | category | flops | bytes accessed | tf_op | source)
XLA Modules:
  0.0 36.1 jit_solution(18242712682881057282)
XLA Ops:
  0.7 34.1 %shard_map.136 = f32[2,9,128]{2,1,0:T(8,128)} custom-call(s32[3,1,1536]{2,1,0:T(1,128)} %bitcast.16, s32[1,256]{1,0:T(1,128)} %bitcast.23, f32[1,1,768]{2,1,0:T(1,128)} %bitcast.21, s32[1,1]{1,0:T(1,128)} %bitcast.13.refs_3_, f32[3,1,256]{2,1,0:T(1,128)} %bitcast.22, s32[1,2]{1,0:T(1,128)} %bitcast.25, f32[8,256]{1,0:T(8,128)} %bitcast.17, ...), custom_call_target="tpu_custom_call" | custom-call | tf_op jit(solution)/shard_map/pallas_call | solution.py:561
  34.7 1.3 %copy.15 = f32[1,1,1,2,9,128]{5,3,4,2,1,0:T(2,128)} copy(f32[1,1,1,2,9,128]{5,4,3,2,1,0:T(8,128)} %bitcast.15) | data formatting | bytes 18432 | tf_op jit(solution)/shard_map/broadcast_in_dim | solution.py:589

commit v3 on v2

--- a/solution.py
+++ b/solution.py
@@ -378,6 +378,12 @@
     return step % size
 
 
+def owners_of_pieces(sizes):
+    xs, ys, zs = sizes
+    steps = {(x % xs, y % ys, z) for x in (-1, 0, 1) for y in (-1, 0, 1) for z in range(zs)}
+    return sorted(steps - {(0, 0, 0)})
+
+
 def kernel(
     sizes,
     *refs,
@@ -388,8 +394,8 @@
     pair, kind, pos, live_ref, vel, owner_ref = loaded[:6]
     weights = loaded[6:]
     w_scratch, store = scratch[:17], scratch[17:33]
-    (mem_t, nbr_t, halo, force_out, force_in, move_out, move_in,
-     pos_send, pos_recv, force_send, force_recv, move_send, move_recv, load_sem) = scratch[33:47]
+    (mem_t, nbr_t, halo, force_out, force_in, info_out, info_in,
+     pos_send, pos_recv, force_send, force_recv, info_send, info_recv, load_sem) = scratch[33:47]
     loads = [
         pltpu.make_async_copy(source, target, load_sem.at[k])
         for k, (source, target) in enumerate(zip(sources, loaded))
@@ -409,10 +415,7 @@
     leader = [first[(s[0] % xs, s[1] % ys, s[2] % zs)] for s in slots]
     home = first[(0, 0, 0)]
     leaders = [k for k in first.values() if k != home]
-    partners = {(s[0] % xs, s[1] % ys, s[2] % zs) for s in (slots[k] for k in leaders)}
-    partners |= {((-x) % xs, (-y) % ys, (-z) % zs) for x, y, z in partners}
-    partners |= {(0, 0, z) for z in range(1, zs)}
-    partners = sorted(partners)
+    partners = owners_of_pieces(sizes)
 
     barrier = pltpu.get_barrier_semaphore()
     for step in partners:
@@ -443,6 +446,18 @@
     near = jnp.concatenate([near[0:8] + near[8:16] + near[16:24], near[24:32]], axis=0)
     for load in loads[3:]:
         load.wait()
+    info_out[0, :, : 3 * atoms] = pos[0]
+    for m in range(3):
+        info_out[0, :, (3 + m) * atoms : (4 + m) * atoms] = vel[m]
+    info_out[0, :, 6 * atoms : 7 * atoms] = kind[...].astype(F32)
+    info_out[0, :, 7 * atoms :] = jnp.concatenate(
+        [jnp.broadcast_to(owner_ref[:, b : b + 1], (1, 128)) for b in range(atoms // 128)], axis=1
+    ).astype(F32)
+    info_copies = [
+        push(j, info_out.at[0], info_in.at[j], info_send, info_recv, (0, 0, -j)) for j in range(1, zs)
+    ]
+    for copy in info_copies:
+        copy.start()
     prepare(weights, w_scratch)
 
     for copy in pos_copies:
@@ -460,63 +475,52 @@
     )
 
     members = {k: [j for j in range(SLOTS) if leader[j] == k] for k in leaders + [home]}
-
-    def piece(k):
+    pieces = {}
+    for step, k in first.items():
         parts = []
         for m in range(3):
             row = by_slot[32 * m + k : 32 * m + k + 1]
             for j in members[k][1:]:
                 row = row + by_slot[32 * m + j : 32 * m + j + 1]
-            parts.append(row)
-        return parts
+            parts.append(row - by_centre[m : m + 1] if k == home else row)
+        pieces[step] = parts
+    nothing = [jnp.zeros((1, atoms), F32)] * 3
 
     force_copies = []
-    for k in leaders:
-        for m, row in enumerate(piece(k)):
-            force_out[k, :, m * atoms : (m + 1) * atoms] = row
-        copy = push(k, force_out.at[k], force_in.at[k], force_send, force_recv, slots[k])
+    for t, (x, y, z) in enumerate(partners):
+        for j in range(zs):
+            for m, row in enumerate(pieces.get((x, y, (z + j) % zs), nothing)):
+                lane = (3 * j + m) * atoms
+                force_out[t, :, lane : lane + atoms] = row
+        copy = push(t, force_out.at[t], force_in.at[t], force_send, force_recv, (x, y, z))
         copy.start()
         force_copies.append(copy)
-    total = jnp.concatenate(piece(home), axis=0) - by_centre[0:3]
-    inverse_mass = 1.0 / (1.0 + kind[...].astype(F32))
-    velocity = jnp.concatenate([vel[0], vel[1], vel[2]], axis=0)
-    for copy in force_copies:
+    for copy in info_copies + force_copies:
         copy.wait()
-    arrived = force_in[leaders[0]]
-    for k in leaders[1:]:
-        arrived = arrived + force_in[k]
-    total = total + jnp.concatenate(
-        [arrived[:, m * atoms : (m + 1) * atoms] for m in range(3)], axis=0
-    )
-    forces = -total
-    new_vel = velocity + TIME_STEP * forces * inverse_mass
-    new_pos = here + TIME_STEP * new_vel
-    state = jnp.concatenate([new_pos, new_vel, forces], axis=0)
-    blocks = atoms // 128
-    depth = float(atoms // 64)
+    arrived = force_in[0]
+    for t in range(1, len(partners)):
+        arrived = arrived + force_in[t]
     is_z = (lax.broadcasted_iota(jnp.int32, (9, 128), 0) == 2).astype(F32)
-
-    def block_for(target):
+    myself = me[2].astype(F32)
+    for j in range(zs):
+        about = info_out[0] if j == 0 else info_in[j]
+        part = pieces.get((0, 0, j), nothing)
+        forces = -jnp.concatenate(
+            [part[m] + arrived[:, (3 * j + m) * atoms : (3 * j + m + 1) * atoms] for m in range(3)], axis=0
+        )
+        place = jnp.concatenate([about[:, m * atoms : (m + 1) * atoms] for m in range(3)], axis=0)
+        speed = jnp.concatenate([about[:, (3 + m) * atoms : (4 + m) * atoms] for m in range(3)], axis=0)
+        new_vel = speed + TIME_STEP * forces * (1.0 / (1.0 + about[:, 6 * atoms : 7 * atoms]))
+        new_pos = place + TIME_STEP * new_vel
+        state = jnp.concatenate([new_pos, new_vel, forces], axis=0)
+        source = lax.rem(me[2] + j, zs)
+        lift = is_z * ((source - me[2]).astype(F32) * float(atoms // 64))
         result = jnp.zeros((9, 128), F32)
-        lift = (me[2] - target).astype(F32) * depth
-        for b in range(blocks):
-            mine = jnp.broadcast_to(owner_ref[:, b : b + 1], (9, 128)) == target
-            result = result + jnp.where(mine, state[:, 128 * b : 128 * b + 128] + is_z * lift, 0.0)
-        return result
-
-    move_copies = []
-    for z in range(1, zs):
-        target = lax.rem(me[2] + z, zs)
-        move_out[z] = block_for(target)
-        copy = push(z, move_out.at[z], move_in.at[z], move_send, move_recv, (0, 0, z))
-        copy.start()
-        move_copies.append(copy)
-    out[me[2]] = block_for(me[2])
-    for copy in move_copies:
-        copy.wait()
-    for z in range(1, zs):
-        source = lax.rem(me[2] + zs - z, zs)
-        out[source] = move_in[z]
+        for b in range(atoms // 128):
+            owner = about[:, 7 * atoms + 128 * b : 7 * atoms + 128 * b + 128]
+            mine = jnp.broadcast_to(owner, (9, 128)) == myself
+            result = result + jnp.where(mine, state[:, 128 * b : 128 * b + 128] + lift, 0.0)
+        out[source] = result
 
 
 def per_device(
@@ -542,6 +546,7 @@
     ch = vector_weight.shape[0]
     zs = sizes[2]
     dma = pltpu.SemaphoreType.DMA
+    senders = len(owners_of_pieces(sizes))
     operands = (
         pair_table.reshape(3, 1, count),
         species.reshape(1, atoms),
@@ -569,14 +574,14 @@
             pltpu.VMEM((atoms, count), BF16),
             pltpu.VMEM((atoms, count), BF16),
             pltpu.VMEM((SLOTS, 1, 3 * atoms), F32),
-            pltpu.VMEM((SLOTS, 1, 3 * atoms), F32),
-            pltpu.VMEM((SLOTS, 1, 3 * atoms), F32),
-            pltpu.VMEM((zs, 9, 128), F32),
-            pltpu.VMEM((zs, 9, 128), F32),
+            pltpu.VMEM((senders, 1, 3 * zs * atoms), F32),
+            pltpu.VMEM((senders, 1, 3 * zs * atoms), F32),
+            pltpu.VMEM((1, 1, 8 * atoms), F32),
+            pltpu.VMEM((zs, 1, 8 * atoms), F32),
             dma((SLOTS,)),
             dma((SLOTS,)),
-            dma((SLOTS,)),
-            dma((SLOTS,)),
+            dma((senders,)),
+            dma((senders,)),
             dma((zs,)),
             dma((zs,)),
             dma((14,)),

time: 36.3 us -> 34.4 us (0.948); the launches traced: 36.1 us -> 33.7 us
  Pallas kernels: 34.1 us -> 31.7 us
    pallas_call x1, Pallas kernels: 34.1 us -> 31.7 us  [per_device(): pl.pallas_call(functools.partial(kernel, sizes), out_shape=jax.ShapeDtype...]
where the time goes in v3:
time: 34.4 us; the launch traced here: 33.7 us
  Pallas kernels  31.7 us (92%)
  local copies, waits for them, and re-layouts  1.32 us (4%)
  between operations  0.66 us (2%)
    pallas_call x1, Pallas kernels, per_device(): pl.pallas_call(functools.partial(kernel, sizes), out_shape=jax.ShapeDtype...  31.7 us
    broadcast_in_dim x1, local copies, waits for them, and re-layouts, per_device(): return result[None, None, None]  1.32 us

profile of v3, /device:TPU:0, one launch (start us, length us, event | category | flops | bytes accessed | tf_op | source)
XLA Modules:
  0.0 33.7 jit_solution(17215859040076614195)
XLA Ops:
  0.7 31.7 %shard_map.136 = f32[2,9,128]{2,1,0:T(8,128)} custom-call(s32[3,1,1536]{2,1,0:T(1,128)} %bitcast.16, s32[1,256]{1,0:T(1,128)} %bitcast.23, f32[1,1,768]{2,1,0:T(1,128)} %bitcast.21, s32[1,1]{1,0:T(1,128)} %bitcast.13.refs_3_, f32[3,1,256]{2,1,0:T(1,128)} %bitcast.22, s32[1,2]{1,0:T(1,128)} %bitcast.25, f32[8,256]{1,0:T(8,128)} %bitcast.17, ...), custom_call_target="tpu_custom_call" | custom-call | tf_op jit(solution)/shard_map/pallas_call | solution.py:566
  32.4 1.3 %copy.15 = f32[1,1,1,2,9,128]{5,3,4,2,1,0:T(2,128)} copy(f32[1,1,1,2,9,128]{5,4,3,2,1,0:T(8,128)} %bitcast.15) | data formatting | bytes 18432 | tf_op jit(solution)/shard_map/broadcast_in_dim | solution.py:594
